TPU v7x, 128 devices: a whole 4x4x4 slice. The times are simulated.
128 devices in a mesh: row: 4 (over y_hi, core), col: 4 (over z), dp: 8 (over y_lo, x).
Axes of the slice: x: 4, y: 4 (y_hi: 2, y_lo: 2; y = y_hi * 2 + y_lo), z: 4, core: 2. Of those that a mesh axis runs over, the one named last changes fastest.
Arguments:
- observed: bfloat16 [4096, 2048], P(('row', 'dp'), 'col'), may hold values from -6 to 6
- next_observed: bfloat16 [4096, 2048], P(('row', 'dp'), 'col'), may hold values from -6 to 6
- actions: bfloat16 [4096, 128], P(('row', 'dp')), may hold values from -1 to 1
- next_mean: bfloat16 [4096, 128], P(('row', 'dp')), may hold values from -1.1953125 to 1.1953125
- policy_noise: float32 [4096, 128], P(('row', 'dp')), may hold values from -1.5 to 1.5
- rewards: bfloat16 [4096], P(('row', 'dp')), may hold values from -5 to 5
- discounts: bfloat16 [4096], P(('row', 'dp')), may hold values from 0.5 to 0.98828125
- actor_flags: int32 [4096], P(('row', 'dp')), may hold values 0 or 1
- critic_in: float32 [2, 2048, 2048], P(None, 'col', 'row'), may hold values from -0.125 to 0.125
- critic_act: float32 [2, 128, 2048], P(None, None, 'col'), may hold values from -0.5 to 0.5
- critic_head: float32 [2, 2048], P(None, 'row'), may hold values from -0.125 to 0.125
- target_in: float32 [2, 2048, 2048], P(None, 'col', 'row'), may hold values from -0.125 to 0.125
- target_act: float32 [2, 128, 2048], P(None, None, 'col'), may hold values from -0.5 to 0.5
- target_head: float32 [2, 2048], P(None, 'row'), may hold values from -0.125 to 0.125
Outputs:
- new_in: float32 [2, 2048, 2048], P(None, 'col', 'row')
- new_act: float32 [2, 128, 2048], P(None, None, 'col')
- new_head: float32 [2, 2048], P(None, 'row')
- new_target_in: float32 [2, 2048, 2048], P(None, 'col', 'row')
- new_target_act: float32 [2, 128, 2048], P(None, None, 'col')
- new_target_head: float32 [2, 2048], P(None, 'row')
- temporal_errors: float32 [2, 4096], P(None, ('row', 'dp'))
- action_slope: float32 [4096, 128], P(('row', 'dp'))
All inputs are finite; a program needn't handle non-finite values. No bound on the sum of `actor_flags` on one device may be relied on, other than what follows from the above.
Results may differ from a plain program's by a relative error of at most 0.008.
Values may be sent and summed in bfloat16 or wider, within the bound.
No kernel may reach another device: no remote copies, remote signals or barrier semaphores. Data moves between devices by JAX's collectives and lax.ppermute only.
A program may use at most 128 MiB of HBM per device.

v0:
```python
import math
import jax
import jax.numpy as jnp
from jax import lax
from jax.sharding import PartitionSpec as P

noise_clip = 0.5
matrix_rate = 0.004
head_rate = 0.0001
blend_rate = 0.005


def in_one_piece(arrays, axis, dim, along):
    widths = [math.prod(a.shape[along:]) for a in arrays]
    both = jnp.concatenate(
        [a.reshape(*a.shape[:along], w) for a, w in zip(arrays, widths)], axis=along
    )
    whole = lax.all_gather(both, axis, axis=dim, tiled=True)
    blocks = jnp.split(whole, [sum(widths[:k]) for k in range(1, len(widths))], axis=along)
    return tuple(
        (b.reshape(*whole.shape[:along], *a.shape[along:]) for a, b in zip(arrays, blocks))
    )


def in_one_piece_2(arrays, axis, dim, along):
    ends, at = ([], 0)
    for a in arrays[:-1]:
        at += a.shape[along]
        ends.append(at)
    both = jnp.concatenate(arrays, axis=along)
    return tuple(
        jnp.split(lax.psum_scatter(both, axis, scatter_dimension=dim, tiled=True), ends, axis=along)
    )


def sent_to_all(x, axis):
    copies = jnp.broadcast_to(x, (lax.axis_size(axis), *x.shape))
    return lax.all_to_all(copies, axis, split_axis=0, concat_axis=0, tiled=True)


def taken_together(x, axis):
    return sent_to_all(x, axis).sum(axis=0)


def packed_total(arrays, axis):
    ends = [0]
    for a in arrays:
        ends.append(ends[-1] + a.size)
    running = taken_together(jnp.concatenate([a.ravel() for a in arrays]), axis)
    return tuple((running[b:e].reshape(a.shape) for a, b, e in zip(arrays, ends, ends[1:])))


def in_one_piece_3(arrays, axis, dim, along):
    both = jnp.concatenate(arrays, axis=along)
    whole, at, gathered = (lax.all_gather(both, axis, axis=dim, tiled=True), 0, [])
    for a in arrays:
        gathered.append(lax.slice_in_dim(whole, at, at + a.shape[along], axis=along))
        at += a.shape[along]
    return tuple(gathered)


def rows_first(arrays, axis, dims):
    turned = [jnp.moveaxis(a, dim, 0) for a, dim in zip(arrays, dims)]
    widths = [t[0].size for t in turned]
    both = jnp.concatenate([t.reshape(-1, w) for t, w in zip(turned, widths)], axis=1)
    whole = lax.all_gather(both, axis, axis=0, tiled=True)
    blocks = jnp.split(whole, [sum(widths[:k]) for k in range(1, len(widths))], axis=1)
    return tuple(
        (
            jnp.moveaxis(b.reshape(-1, *t.shape[1:]), 0, dim)
            for b, t, dim in zip(blocks, turned, dims)
        )
    )


def silu_slope(preact):
    sigma = jax.nn.sigmoid(preact)
    return sigma * (1.0 + preact * (1.0 - sigma))


def embed(states, moves, weight_act):
    summed = states.astype(jnp.float32) + jnp.dot(
        moves, weight_act.astype(jnp.bfloat16), preferred_element_type=jnp.float32
    )
    return summed.astype(jnp.bfloat16)


def contract_rows(left, right):
    return lax.dot_general(
        left, right, (((0,), (0,)), ((), ())), preferred_element_type=jnp.float32
    )


def on_device(
    observed,
    next_observed,
    actions,
    next_mean,
    policy_noise,
    rewards,
    discounts,
    actor_flags,
    critic_in,
    critic_act,
    critic_head,
    target_in,
    target_act,
    target_head,
):
    noisy = jnp.clip(
        next_mean.astype(jnp.float32) + jnp.clip(policy_noise, -noise_clip, noise_clip), -1.0, 1.0
    ).astype(jnp.bfloat16)
    states, next_states, moves, next_moves, group_rewards, group_discounts = in_one_piece(
        (observed, next_observed, actions, noisy, rewards, discounts), "row", 0, 1
    )
    inner = [critic_in[which].astype(jnp.bfloat16) for which in range(2)]
    online = [embed(states, moves, critic_act[which]) for which in range(2)]
    shadow = [embed(next_states, next_moves, target_act[which]) for which in range(2)]
    partials = [
        jnp.dot(online[which], inner[which], preferred_element_type=jnp.float32)
        for which in range(2)
    ]
    partials += [
        jnp.dot(
            shadow[which], target_in[which].astype(jnp.bfloat16), preferred_element_type=jnp.float32
        )
        for which in range(2)
    ]
    total_rows = states.shape[0]
    preacts = tuple(
        (
            part.astype(jnp.float32)
            for part in in_one_piece_2(
                (
                    partials[0].astype(jnp.bfloat16),
                    partials[1].astype(jnp.bfloat16),
                    partials[2].astype(jnp.bfloat16),
                    partials[3].astype(jnp.bfloat16),
                ),
                "col",
                0,
                1,
            )
        )
    )
    row_count = total_rows // lax.axis_size("col")
    first_row = lax.axis_index("col") * row_count
    share_rewards = lax.dynamic_slice_in_dim(group_rewards, first_row, row_count).astype(
        jnp.float32
    )
    share_discounts = lax.dynamic_slice_in_dim(group_discounts, first_row, row_count).astype(
        jnp.float32
    )
    heads = [critic_head[0], critic_head[1], target_head[0], target_head[1]]
    hiddens = [jax.nn.silu(preacts[which]) for which in range(4)]
    value_terms = [
        jnp.dot(hiddens[which], heads[which], precision=lax.Precision.HIGHEST) for which in range(4)
    ]
    values = packed_total((value_terms[0], value_terms[1], value_terms[2], value_terms[3]), "row")
    goal = share_rewards + share_discounts * jnp.minimum(values[2], values[3])
    errors = [values[0] - goal, values[1] - goal]
    slopes = [
        (heads[which] * silu_slope(preacts[which])).astype(jnp.bfloat16) for which in range(2)
    ]
    head_grads = [
        jnp.dot(2.0 * errors[which], hiddens[which], precision=lax.Precision.HIGHEST)
        for which in range(2)
    ]
    slopes = list(in_one_piece_3((slopes[0], slopes[1]), "col", 0, 1))
    errors = list(rows_first((errors[0], errors[1]), "col", (0, 0)))
    head_grads = list(packed_total((head_grads[0], head_grads[1]), "col"))
    deltas = [
        (2.0 * errors[which][:, None] * slopes[which].astype(jnp.float32)).astype(jnp.bfloat16)
        for which in range(2)
    ]
    back_terms = [
        lax.dot_general(
            slopes[which],
            inner[which],
            (((1,), (1,)), ((), ())),
            preferred_element_type=jnp.float32,
        )
        for which in range(2)
    ]
    grad_ins = [contract_rows(online[which], deltas[which]) for which in range(2)]
    own_rows = observed.shape[0]
    own_first = lax.axis_index("row") * own_rows
    own_errors = [
        lax.dynamic_slice_in_dim(errors[which], own_first, own_rows) for which in range(2)
    ]
    backs = lax.psum((back_terms[0], back_terms[1]), "row")
    grad_embedded = [
        (2.0 * errors[which][:, None] * backs[which]).astype(jnp.bfloat16) for which in range(2)
    ]
    grad_acts = [contract_rows(moves, grad_embedded[which]) for which in range(2)]
    mine = lax.dynamic_slice_in_dim(backs[0], own_first, own_rows).astype(jnp.bfloat16)
    push_term = lax.dot_general(
        mine,
        critic_act[0].astype(jnp.bfloat16),
        (((1,), (1,)), ((), ())),
        preferred_element_type=jnp.float32,
    )
    action_slope = taken_together(push_term, "col") * actor_flags.astype(jnp.float32)[:, None]
    temporal_errors = jnp.stack(own_errors)
    olds = [
        critic_in[0],
        critic_in[1],
        critic_act[0],
        critic_act[1],
        critic_head[0],
        critic_head[1],
    ]
    rates = [matrix_rate, matrix_rate, matrix_rate, matrix_rate, head_rate, head_rate]
    summed = (
        lax.psum(grad_ins[0].astype(jnp.bfloat16), "dp").astype(jnp.float32),
        lax.psum(grad_ins[1].astype(jnp.bfloat16), "dp").astype(jnp.float32),
        lax.psum(grad_acts[0].astype(jnp.bfloat16), "dp").astype(jnp.float32),
        lax.psum(grad_acts[1].astype(jnp.bfloat16), "dp").astype(jnp.float32),
        lax.psum(head_grads[0].astype(jnp.bfloat16), "dp").astype(jnp.float32),
        lax.psum(head_grads[1].astype(jnp.bfloat16), "dp").astype(jnp.float32),
    )
    fresh = [olds[which] - rates[which] * summed[which] for which in range(6)]
    new_in = jnp.stack([fresh[0], fresh[1]])
    new_act = jnp.stack([fresh[2], fresh[3]])
    new_head = jnp.stack([fresh[4], fresh[5]])
    new_target_in = blend_rate * new_in + (1.0 - blend_rate) * target_in
    new_target_act = blend_rate * new_act + (1.0 - blend_rate) * target_act
    new_target_head = blend_rate * new_head + (1.0 - blend_rate) * target_head
    return (
        new_in,
        new_act,
        new_head,
        new_target_in,
        new_target_act,
        new_target_head,
        temporal_errors,
        action_slope,
    )


def solution(mesh):
    return jax.shard_map(
        on_device,
        mesh=mesh,
        in_specs=(
            P(("row", "dp"), "col"),
            P(("row", "dp"), "col"),
            P(("row", "dp"), None),
            P(("row", "dp"), None),
            P(("row", "dp"), None),
            P(("row", "dp")),
            P(("row", "dp")),
            P(("row", "dp")),
            P(None, "col", "row"),
            P(None, None, "col"),
            P(None, "row"),
            P(None, "col", "row"),
            P(None, None, "col"),
            P(None, "row"),
        ),
        out_specs=(
            P(None, "col", "row"),
            P(None, None, "col"),
            P(None, "row"),
            P(None, "col", "row"),
            P(None, None, "col"),
            P(None, "row"),
            P(None, ("row", "dp")),
            P(("row", "dp"), None),
        ),
        check_vma=False,
    )
```

profile of v0, /device:TPU:0, one launch (start us, length us, event | category | flops | bytes accessed | tf_op | source)
XLA Modules:
  0.0 270.5 jit_solution(15028285660459501925)
XLA Ops:
  9.6 1.8 concatenate.18
  12.7 2.8 %convert.15 = bf16[2,512,512]{2,1,0:T(8,128)(2,1)} convert(f32[2,512,512]{2,1,0:T(8,128)} %param.25) | non-fusion elementwise | flops 524288 | bytes 3145728 | tf_op jit(solution)/shard_map/convert.6
  15.5 21.6 %all-gather.3.cloned.1.call-done = bf16[512,1282]{1,0:T(8,128)(2,1)} async-done(((bf16[128,1282]{1,0:T(8,128)(2,1)}), bf16[512,1282]{1,0:T(8,128)(2,1)}) %all-gather.3.cloned.1.call-update) | async-done | bytes 1312784 | tf_op jit(solution)/shard_map/all_gather | solution.py:18
  37.1 1.4 fusion
  38.5 1.3 convolution_convert_fusion.5
  39.8 1.4 fusion.1
  42.0 1.3 convolution_convert_fusion.4
  43.3 2.7 %convolution_convert_fusion.2 = bf16[512,512]{0,1:T(8,128)(2,1)} fusion(bf16[2,512,512]{2,1,0:T(8,128)(2,1)} %convert.15, bf16[512,1282]{1,0:T(8,128)(2,1)} %all-gather.3.cloned.1.call-done, bf16[2,128,512]{2,1,0:T(8,128)(2,1)S(1)} %convert.14), kind=kOutput, calls=%fused_computation.13 | convolution fusion | flops 336592896 | bytes 1835008 | tf_op jit(solution)/shard_map/dot_general | solution.py:124
  46.0 2.7 %convolution_convert_fusion.3 = bf16[512,512]{0,1:T(8,128)(2,1)} fusion(bf16[2,512,512]{2,1,0:T(8,128)(2,1)} %convert.15, bf16[512,1282]{1,0:T(8,128)(2,1)} %all-gather.3.cloned.1.call-done, bf16[2,128,512]{2,1,0:T(8,128)(2,1)S(1)} %convert.14), kind=kOutput, calls=%fused_computation.14 | convolution fusion | flops 336592896 | bytes 1835008 | tf_op jit(solution)/shard_map/dot_general | solution.py:124
  48.7 3.0 %pad_maximum_fusion = bf16[512,2048]{0,1:T(8,128)(2,1)} fusion(bf16[512,512]{0,1:T(8,128)(2,1)} %convolution_convert_fusion.2, bf16[512,512]{0,1:T(8,128)(2,1)} %convolution_convert_fusion.3, bf16[512,512]{0,1:T(8,128)(2,1)} %convolution_convert_fusion.4, bf16[512,512]{0,1:T(8,128)(2,1)} %convolution_convert_fusion.5), kind=kLoop, calls=%fused_computation | loop fusion | flops 8388608 | bytes 4194304 | tf_op jit(solution)/shard_map/concatenate | solution.py:30
  51.7 3.9 %copy.48 = bf16[512,2048]{1,0:T(8,128)(2,1)} copy(bf16[512,2048]{0,1:T(8,128)(2,1)} %pad_maximum_fusion) | data formatting | bytes 4194304
  56.3 28.8 %reduce-scatter.4.cloned.1.call-done = bf16[128,2048]{1,0:T(8,128)(2,1)} async-done(((bf16[512,2048]{1,0:T(8,128)(2,1)}), bf16[128,2048]{1,0:T(8,128)(2,1)}) %reduce-scatter.4.cloned.1.call-update) | async-done | bytes 524304 | tf_op jit(solution)/shard_map/reduce_scatter | solution.py:32
  87.1 1.3 convolution_bitcast_fusion.3
  88.4 1.3 convolution_bitcast_fusion.1
  91.1 4.3 %all-to-all-start = ((f32[4,1,512]{2,1,0:T(1,128)}), f32[4,1,512]{2,1,0:T(1,128)S(1)}, u32[]{:S(2)}, u32[]{:S(2)}) async-start(f32[4,1,512]{2,1,0:T(1,128)} %broadcast_in_dim.10), calls=%async_computation | async-start | bytes 16384 | tf_op jit(solution)/shard_map/all_to_all | solution.py:38
  96.6 4.1 %all-to-all-done = f32[4,1,512]{2,1,0:T(1,128)S(1)} async-done(((f32[4,1,512]{2,1,0:T(1,128)}), f32[4,1,512]{2,1,0:T(1,128)S(1)}, u32[]{:S(2)}, u32[]{:S(2)}) %all-to-all-start) | async-done | bytes 8224 | tf_op jit(solution)/shard_map/all_to_all | solution.py:38
  100.7 10.5 %all-gather.5.cloned.1.call-done = bf16[512,1024]{1,0:T(8,128)(2,1)} async-done(((bf16[128,1024]{1,0:T(8,128)(2,1)}), bf16[512,1024]{1,0:T(8,128)(2,1)}) %all-gather.5.cloned.1.call-update) | async-done | bytes 1048592 | tf_op jit(solution)/shard_map/all_gather | solution.py:55
  111.2 2.6 fusion.13
  113.8 1.4 fusion.10
  118.3 3.5 %all-to-all-start.1 = ((f32[4,1,1024]{2,1,0:T(1,128)}), f32[4,1,1024]{2,1,0:T(1,128)S(1)}, u32[]{:S(2)}, u32[]{:S(2)}) async-start(f32[4,1,1024]{2,1,0:T(1,128)} %broadcast_in_dim.11), calls=%async_computation.1 | async-start | bytes 32768 | tf_op jit(solution)/shard_map/all_to_all | solution.py:38
  121.9 10.2 %all_gather.10 = f32[512,2]{0,1:T(2,128)S(1)} all-gather(f32[128,2]{0,1:T(2,128)S(1)} %pad_maximum_fusion.7), channel_id=1, replica_groups=mesh['row'=4,'col'=4,'dp'=8] {'col'}, dimensions={0}, use_global_device_ids=true | all-gather | bytes 5120 | tf_op jit(solution)/shard_map/all_gather | solution.py:66
  132.7 2.6 convolution_convert_fusion
  135.3 1.3 convolution_convert_fusion.1
  136.6 38.3 %all-reduce.6.cloned.1.call-done = (f32[512,512]{1,0:T(8,128)}, f32[512,512]{1,0:T(8,128)}) async-done(((f32[512,512]{1,0:T(8,128)}, f32[512,512]{1,0:T(8,128)}), (f32[512,512]{1,0:T(8,128)}, f32[512,512]{1,0:T(8,128)})) %all-reduce.6.cloned.1.call-update) | async-done | bytes 2097168 | tf_op jit(solution)/shard_map/psum | solution.py:191
  175.0 2.3 convolution_convert_fusion.6
  177.3 2.3 convolution_convert_fusion.7
  179.6 18.8 %all-reduce.1 = (bf16[512]{0:T(512)(128)(2,1)S(1)}, bf16[512]{0:T(512)(128)(2,1)S(1)}) all-reduce(bf16[512]{0:T(512)(128)(2,1)S(1)} %get-tuple-element.39, bf16[512]{0:T(512)(128)(2,1)S(1)} %get-tuple-element.38), channel_id=1, replica_groups=mesh['row'=4,'col'=4,'dp'=8] {'dp'}, use_global_device_ids=true, to_apply=%region_10.11 | all-reduce | flops 1024 | bytes 4096 | tf_op jit(solution)/shard_map/psum | solution.py:220
  200.3 4.4 %all-to-all-start.2 = ((f32[4,128,128]{2,1,0:T(8,128)}), f32[4,128,128]{2,1,0:T(8,128)S(1)}, u32[]{:S(2)}, u32[]{:S(2)}) async-start(f32[4,128,128]{2,1,0:T(8,128)} %broadcast_in_dim.12), calls=%async_computation.2 | async-start | bytes 524288 | tf_op jit(solution)/shard_map/all_to_all | solution.py:38
  205.3 6.1 %all-to-all-done.2 = f32[4,128,128]{2,1,0:T(8,128)S(1)} async-done(((f32[4,128,128]{2,1,0:T(8,128)}), f32[4,128,128]{2,1,0:T(8,128)S(1)}, u32[]{:S(2)}, u32[]{:S(2)}) %all-to-all-start.2) | async-done | bytes 262176 | tf_op jit(solution)/shard_map/all_to_all | solution.py:38
  212.1 45.5 %all-reduce.8.cloned.1.call-done = (bf16[512,512]{1,0:T(8,128)(2,1)}, bf16[512,512]{1,0:T(8,128)(2,1)}, bf16[128,512]{1,0:T(8,128)(2,1)}, bf16[128,512]{1,0:T(8,128)(2,1)}) async-done(((bf16[512,512]{1,0:T(8,128)(2,1)}, bf16[512,512]{1,0:T(8,128)(2,1)}, bf16[128,512]{1,0:T(8,128)(2,1)}, bf16[128,512]{1,0:T(8,128)(2,1)}), (bf16[512,512]{1,0:T(8,128)(2,1)}, bf16[512,512]{1,0:T(8,128)(2,1)}, ...) | async-done | bytes 1310736 | tf_op jit(solution)/shard_map/psum | solution.py:216
  260.2 1.2 copy-done.1
  261.4 2.5 multiply_add_fusion
  (74 shorter events, 19.3 us)
Async XLA Ops:
  7.2 29.9 %all-gather.3.cloned.1.call-start = ((), (), s32[]{:S(2)}) async-start(), calls=%async_computation.4 | async-start | bytes 1802240 | tf_op jit(solution)/shard_map/all_gather | solution.py:18
  11.4 25.6 %copy-start.2 = (f32[2,128,512]{2,1,0:T(8,128)S(1)}, f32[2,128,512]{2,1,0:T(8,128)}, u32[]{:S(2)}) copy-start(f32[2,128,512]{2,1,0:T(8,128)} %param.23) | copy-start | bytes 1572868
  11.5 73.6 %reduce-scatter.4.cloned.1.call-start = ((), (), s32[]{:S(2)}) async-start(), calls=%async_computation.6 | async-start | bytes 2621440 | tf_op jit(solution)/shard_map/reduce_scatter | solution.py:32
  12.6 25.8 %copy-start = (f32[2,512,512]{2,1,0:T(8,128)S(1)}, f32[2,512,512]{2,1,0:T(8,128)}, u32[]{:S(2)}) copy-start(f32[2,512,512]{2,1,0:T(8,128)} %param.22) | copy-start | bytes 6291460
  41.2 0.8 copy-start.3
  55.6 0.7 copy-start.10
  55.6 31.4 %copy-start.12 = (s32[128]{0:T(128)S(1)}, s32[128]{0:T(128)}, u32[]{:S(2)}) copy-start(s32[128]{0:T(128)} %param.21) | copy-start | bytes 1540
  55.6 32.8 %copy-start.11 = (f32[2,512]{1,0:T(2,128)S(1)}, f32[2,512]{1,0:T(2,128)}, u32[]{:S(2)}) copy-start(f32[2,512]{1,0:T(2,128)} %param.27) | copy-start | bytes 12292
  55.6 55.6 %all-gather.5.cloned.1.call-start = ((), (), s32[]{:S(2)}) async-start(), calls=%async_computation.5 | async-start | bytes 1310720 | tf_op jit(solution)/shard_map/all_gather | solution.py:55
  87.0 2.6 copy-start.9
  91.1 9.6 %all-to-all-start = ((f32[4,1,512]{2,1,0:T(1,128)}), f32[4,1,512]{2,1,0:T(1,128)S(1)}, u32[]{:S(2)}, u32[]{:S(2)}) async-start(f32[4,1,512]{2,1,0:T(1,128)} %broadcast_in_dim.10), calls=%async_computation | async-start | bytes 16384 | tf_op jit(solution)/shard_map/all_to_all | solution.py:38
  95.4 79.6 %all-reduce.6.cloned.1.call-start = ((), (), s32[]{:S(2)}) async-start(), calls=%async_computation.7 | async-start | bytes 4194304 | tf_op jit(solution)/shard_map/psum | solution.py:191
  111.2 2.6 copy-start.5
  118.3 14.3 %all-to-all-start.1 = ((f32[4,1,1024]{2,1,0:T(1,128)}), f32[4,1,1024]{2,1,0:T(1,128)S(1)}, u32[]{:S(2)}, u32[]{:S(2)}) async-start(f32[4,1,1024]{2,1,0:T(1,128)} %broadcast_in_dim.11), calls=%async_computation.1 | async-start | bytes 32768 | tf_op jit(solution)/shard_map/all_to_all | solution.py:38
  121.8 135.7 %all-reduce.8.cloned.1.call-start = ((), (), s32[]{:S(2)}) async-start(), calls=%async_computation.8 | async-start | bytes 2621440 | tf_op jit(solution)/shard_map/psum | solution.py:216
  132.7 2.6 copy-start.6
  179.5 79.2 %copy-start.4 = (f32[2,128,512]{2,1,0:T(8,128)S(1)}, f32[2,128,512]{2,1,0:T(8,128)}, u32[]{:S(2)}) copy-start(f32[2,128,512]{2,1,0:T(8,128)} %param.26) | copy-start | bytes 1572868
  200.3 11.1 %all-to-all-start.2 = ((f32[4,128,128]{2,1,0:T(8,128)}), f32[4,128,128]{2,1,0:T(8,128)S(1)}, u32[]{:S(2)}, u32[]{:S(2)}) async-start(f32[4,128,128]{2,1,0:T(8,128)} %broadcast_in_dim.12), calls=%async_computation.2 | async-start | bytes 524288 | tf_op jit(solution)/shard_map/all_to_all | solution.py:38
  257.6 2.3 copy-start.7
  257.6 2.3 copy-start.8
  259.8 1.6 copy-start.1
Sparse Core Ops, SparseCore 0:
  11.6 25.4 all-gather.2
  55.8 29.2 reduce-scatter.3
  87.4 23.7 all-gather.4
  115.4 59.5 all-reduce.5
  179.7 77.8 all-reduce.7
where the time goes:
time: 271 us; the launch traced here: 270 us
  waiting for transfers between devices  155 us (57%)
  matrix products  30.3 us (11%)
  blocking collectives  29 us (11%)
  other arithmetic  17 us (6%)
  between operations  14 us (5%)
  local copies, waits for them, and re-layouts  13 us (5%)
  starting transfers between devices  12.3 us (5%)
    psum x1, waiting for transfers between devices, on_device(): lax.psum(grad_ins[1].astype(jnp.bfloat16), 'dp').astype(jnp.float32)  45.5 us
    psum x1, waiting for transfers between devices, on_device(): backs = lax.psum((back_terms[0], back_terms[1]), 'row')  38.3 us
    reduce_scatter x1, waiting for transfers between devices, in_one_piece_2(): lax.psum_scatter(both, axis, scatter_dimension=dim, tiled=True)  28.8 us
    all_gather x1, waiting for transfers between devices, in_one_piece(): whole = lax.all_gather(both, axis, axis=dim, tiled=True)  21.6 us
    psum x1, blocking collectives, on_device(): lax.psum(head_grads[1].astype(jnp.bfloat16), 'dp').astype(jnp.float32)  18.8 us
    all_to_all x3, starting transfers between devices, sent_to_all(): return lax.all_to_all(copies, axis, split_axis=0, concat_axis=0, tiled=True)  12.2 us
    all_gather x1, waiting for transfers between devices, in_one_piece_3(): lax.all_gather(both, axis, axis=dim, tiled=True)  10.5 us
    all_gather x1, blocking collectives, rows_first(): whole = lax.all_gather(both, axis, axis=0, tiled=True)  10.2 us
  transfers between devices with their start and end apart: 8, of which 7 were waited for; matrix products, arithmetic and copies ran while one was open for 7% of the time, Pallas kernels for 0%

commit v1 on v0

--- a/solution.py
+++ b/solution.py
@@ -63,7 +63,9 @@
     turned = [jnp.moveaxis(a, dim, 0) for a, dim in zip(arrays, dims)]
     widths = [t[0].size for t in turned]
     both = jnp.concatenate([t.reshape(-1, w) for t, w in zip(turned, widths)], axis=1)
-    whole = lax.all_gather(both, axis, axis=0, tiled=True)
+    whole = jnp.concatenate(
+        lax.all_to_all(jnp.stack([both] * lax.axis_size(axis)), axis, 0, 0), axis=0
+    )
     blocks = jnp.split(whole, [sum(widths[:k]) for k in range(1, len(widths))], axis=1)
     return tuple(
         (

time: 271 us -> 272 us (level)
  blocking collectives: 29 us -> 18.8 us
  waiting for transfers between devices: 155 us -> 161 us
  starting transfers between devices: 12.3 us -> 15.6 us
    all_gather x1 -> x0, blocking collectives: 10.2 us -> none  [rows_first(): whole = lax.all_gather(both, axis, axis=0, tiled=True)]
    all_to_all x3, waiting for transfers between devices: 10.2 us -> 14.8 us  [sent_to_all(): return lax.all_to_all(copies, axis, split_axis=0, concat_axis=0, tiled=True)]
    all_to_all x0 -> x1, starting transfers between devices: none -> 3.49 us  [rows_first(): lax.all_to_all(jnp.stack([both] * lax.axis_size(axis)), axis, 0, 0)]
    all_to_all x0 -> x1, waiting for transfers between devices: none -> 2.88 us  [rows_first(): lax.all_to_all(jnp.stack([both] * lax.axis_size(axis)), axis, 0, 0)]
  transfers between devices with their start and end apart: 8 -> 9, of which waited for: 7 -> 9; matrix products, arithmetic and copies ran while one was open for 7% -> 8% of each run, Pallas kernels for 0% -> 0%
where the time goes in v1:
time: 272 us; the launch traced here: 271 us
  waiting for transfers between devices  161 us (59%)
  matrix products  30.3 us (11%)
  blocking collectives  18.8 us (7%)
  other arithmetic  17 us (6%)
  starting transfers between devices  15.6 us (6%)
  between operations  14 us (5%)
  local copies, waits for them, and re-layouts  13.6 us (5%)
    psum x1, waiting for transfers between devices, on_device(): lax.psum(grad_ins[1].astype(jnp.bfloat16), 'dp').astype(jnp.float32)  45.5 us
    psum x1, waiting for transfers between devices, on_device(): backs = lax.psum((back_terms[0], back_terms[1]), 'row')  37.1 us
    reduce_scatter x1, waiting for transfers between devices, in_one_piece_2(): lax.psum_scatter(both, axis, scatter_dimension=dim, tiled=True)  28.8 us
    all_gather x1, waiting for transfers between devices, in_one_piece(): whole = lax.all_gather(both, axis, axis=dim, tiled=True)  21.6 us
    psum x1, blocking collectives, on_device(): lax.psum(head_grads[1].astype(jnp.bfloat16), 'dp').astype(jnp.float32)  18.8 us
    all_to_all x3, waiting for transfers between devices, sent_to_all(): return lax.all_to_all(copies, axis, split_axis=0, concat_axis=0, tiled=True)  14.8 us
    all_to_all x3, starting transfers between devices, sent_to_all(): return lax.all_to_all(copies, axis, split_axis=0, concat_axis=0, tiled=True)  12 us
    all_gather x1, waiting for transfers between devices, in_one_piece_3(): lax.all_gather(both, axis, axis=dim, tiled=True)  10.5 us
  transfers between devices with their start and end apart: 9, of which 9 were waited for; matrix products, arithmetic and copies ran while one was open for 8% of the time, Pallas kernels for 0%

profile of v1, /device:TPU:0, one launch (start us, length us, event | category | flops | bytes accessed | tf_op | source)
XLA Modules:
  0.0 270.5 jit_solution(12267112437382745263)
XLA Ops:
  9.6 1.8 concatenate.18
  12.7 2.8 %convert.15 = bf16[2,512,512]{2,1,0:T(8,128)(2,1)} convert(f32[2,512,512]{2,1,0:T(8,128)} %param.25) | non-fusion elementwise | flops 524288 | bytes 3145728 | tf_op jit(solution)/shard_map/convert.6
  15.5 21.6 %all-gather.3.cloned.1.call-done = bf16[512,1282]{1,0:T(8,128)(2,1)} async-done(((bf16[128,1282]{1,0:T(8,128)(2,1)}), bf16[512,1282]{1,0:T(8,128)(2,1)}) %all-gather.3.cloned.1.call-update) | async-done | bytes 1312784 | tf_op jit(solution)/shard_map/all_gather | solution.py:18
  37.1 1.4 fusion
  38.5 1.3 convolution_convert_fusion.5
  39.8 1.4 fusion.1
  42.0 1.3 convolution_convert_fusion.4
  43.3 2.7 %convolution_convert_fusion.2 = bf16[512,512]{0,1:T(8,128)(2,1)} fusion(bf16[2,512,512]{2,1,0:T(8,128)(2,1)} %convert.15, bf16[512,1282]{1,0:T(8,128)(2,1)} %all-gather.3.cloned.1.call-done, bf16[2,128,512]{2,1,0:T(8,128)(2,1)S(1)} %convert.14), kind=kOutput, calls=%fused_computation.13 | convolution fusion | flops 336592896 | bytes 1835008 | tf_op jit(solution)/shard_map/dot_general | solution.py:126
  46.0 2.7 %convolution_convert_fusion.3 = bf16[512,512]{0,1:T(8,128)(2,1)} fusion(bf16[2,512,512]{2,1,0:T(8,128)(2,1)} %convert.15, bf16[512,1282]{1,0:T(8,128)(2,1)} %all-gather.3.cloned.1.call-done, bf16[2,128,512]{2,1,0:T(8,128)(2,1)S(1)} %convert.14), kind=kOutput, calls=%fused_computation.14 | convolution fusion | flops 336592896 | bytes 1835008 | tf_op jit(solution)/shard_map/dot_general | solution.py:126
  48.7 3.0 %pad_maximum_fusion = bf16[512,2048]{0,1:T(8,128)(2,1)} fusion(bf16[512,512]{0,1:T(8,128)(2,1)} %convolution_convert_fusion.2, bf16[512,512]{0,1:T(8,128)(2,1)} %convolution_convert_fusion.3, bf16[512,512]{0,1:T(8,128)(2,1)} %convolution_convert_fusion.4, bf16[512,512]{0,1:T(8,128)(2,1)} %convolution_convert_fusion.5), kind=kLoop, calls=%fused_computation | loop fusion | flops 8388608 | bytes 4194304 | tf_op jit(solution)/shard_map/concatenate | solution.py:30
  51.7 3.9 %copy.48 = bf16[512,2048]{1,0:T(8,128)(2,1)} copy(bf16[512,2048]{0,1:T(8,128)(2,1)} %pad_maximum_fusion) | data formatting | bytes 4194304
  56.3 28.8 %reduce-scatter.4.cloned.1.call-done = bf16[128,2048]{1,0:T(8,128)(2,1)} async-done(((bf16[512,2048]{1,0:T(8,128)(2,1)}), bf16[128,2048]{1,0:T(8,128)(2,1)}) %reduce-scatter.4.cloned.1.call-update) | async-done | bytes 524304 | tf_op jit(solution)/shard_map/reduce_scatter | solution.py:32
  87.0 1.3 convolution_bitcast_fusion.3
  91.1 4.3 %all-to-all-start = ((f32[4,1,512]{2,1,0:T(1,128)}), f32[4,1,512]{2,1,0:T(1,128)S(1)}, u32[]{:S(2)}, u32[]{:S(2)}) async-start(f32[4,1,512]{2,1,0:T(1,128)} %broadcast_in_dim.10), calls=%async_computation | async-start | bytes 16384 | tf_op jit(solution)/shard_map/all_to_all | solution.py:38
  96.6 4.1 %all-to-all-done = f32[4,1,512]{2,1,0:T(1,128)S(1)} async-done(((f32[4,1,512]{2,1,0:T(1,128)}), f32[4,1,512]{2,1,0:T(1,128)S(1)}, u32[]{:S(2)}, u32[]{:S(2)}) %all-to-all-start) | async-done | bytes 8224 | tf_op jit(solution)/shard_map/all_to_all | solution.py:38
  100.7 10.5 %all-gather.5.cloned.1.call-done = bf16[512,1024]{1,0:T(8,128)(2,1)} async-done(((bf16[128,1024]{1,0:T(8,128)(2,1)}), bf16[512,1024]{1,0:T(8,128)(2,1)}) %all-gather.5.cloned.1.call-update) | async-done | bytes 1048592 | tf_op jit(solution)/shard_map/all_gather | solution.py:55
  111.2 2.6 fusion.13
  113.8 1.4 fusion.10
  115.9 3.5 %all-to-all-start.1 = ((f32[4,128,2]{1,2,0:T(2,128)}), f32[4,128,2]{1,2,0:T(2,128)S(1)}, u32[]{:S(2)}, u32[]{:S(2)}) async-start(f32[4,128,2]{1,2,0:T(2,128)} %stack.43), calls=%async_computation.1 | async-start | bytes 8192 | tf_op jit(solution)/shard_map/all_to_all | solution.py:67
  121.8 2.9 %all-to-all-done.1 = f32[4,128,2]{1,2,0:T(2,128)S(1)} async-done(((f32[4,128,2]{1,2,0:T(2,128)}), f32[4,128,2]{1,2,0:T(2,128)S(1)}, u32[]{:S(2)}, u32[]{:S(2)}) %all-to-all-start.1) | async-done | bytes 4128 | tf_op jit(solution)/shard_map/all_to_all | solution.py:67
  125.3 3.3 %all-to-all-start.2 = ((f32[4,1,1024]{2,1,0:T(1,128)}), f32[4,1,1024]{2,1,0:T(1,128)S(1)}, u32[]{:S(2)}, u32[]{:S(2)}) async-start(f32[4,1,1024]{2,1,0:T(1,128)} %broadcast_in_dim.11), calls=%async_computation.2 | async-start | bytes 32768 | tf_op jit(solution)/shard_map/all_to_all | solution.py:38
  129.2 4.7 %all-to-all-done.2 = f32[4,1,1024]{2,1,0:T(1,128)S(1)} async-done(((f32[4,1,1024]{2,1,0:T(1,128)}), f32[4,1,1024]{2,1,0:T(1,128)S(1)}, u32[]{:S(2)}, u32[]{:S(2)}) %all-to-all-start.2) | async-done | bytes 16416 | tf_op jit(solution)/shard_map/all_to_all | solution.py:38
  133.9 2.6 convolution_convert_fusion
  136.6 1.3 convolution_convert_fusion.1
  137.9 37.1 %all-reduce.6.cloned.1.call-done = (f32[512,512]{1,0:T(8,128)}, f32[512,512]{1,0:T(8,128)}) async-done(((f32[512,512]{1,0:T(8,128)}, f32[512,512]{1,0:T(8,128)}), (f32[512,512]{1,0:T(8,128)}, f32[512,512]{1,0:T(8,128)})) %all-reduce.6.cloned.1.call-update) | async-done | bytes 2097168 | tf_op jit(solution)/shard_map/psum | solution.py:193
  175.0 2.3 convolution_convert_fusion.6
  177.3 2.3 convolution_convert_fusion.7
  179.6 18.8 %all-reduce.1 = (bf16[512]{0:T(512)(128)(2,1)S(1)}, bf16[512]{0:T(512)(128)(2,1)S(1)}) all-reduce(bf16[512]{0:T(512)(128)(2,1)S(1)} %get-tuple-element.39, bf16[512]{0:T(512)(128)(2,1)S(1)} %get-tuple-element.38), channel_id=1, replica_groups=mesh['row'=4,'col'=4,'dp'=8] {'dp'}, use_global_device_ids=true, to_apply=%region_10.11 | all-reduce | flops 1024 | bytes 4096 | tf_op jit(solution)/shard_map/psum | solution.py:222
  200.3 4.4 %all-to-all-start.3 = ((f32[4,128,128]{2,1,0:T(8,128)}), f32[4,128,128]{2,1,0:T(8,128)S(1)}, u32[]{:S(2)}, u32[]{:S(2)}) async-start(f32[4,128,128]{2,1,0:T(8,128)} %broadcast_in_dim.12), calls=%async_computation.3 | async-start | bytes 524288 | tf_op jit(solution)/shard_map/all_to_all | solution.py:38
  205.3 6.1 %all-to-all-done.3 = f32[4,128,128]{2,1,0:T(8,128)S(1)} async-done(((f32[4,128,128]{2,1,0:T(8,128)}), f32[4,128,128]{2,1,0:T(8,128)S(1)}, u32[]{:S(2)}, u32[]{:S(2)}) %all-to-all-start.3) | async-done | bytes 262176 | tf_op jit(solution)/shard_map/all_to_all | solution.py:38
  212.2 45.5 %all-reduce.8.cloned.1.call-done = (bf16[512,512]{1,0:T(8,128)(2,1)}, bf16[512,512]{1,0:T(8,128)(2,1)}, bf16[128,512]{1,0:T(8,128)(2,1)}, bf16[128,512]{1,0:T(8,128)(2,1)}) async-done(((bf16[512,512]{1,0:T(8,128)(2,1)}, bf16[512,512]{1,0:T(8,128)(2,1)}, bf16[128,512]{1,0:T(8,128)(2,1)}, bf16[128,512]{1,0:T(8,128)(2,1)}), (bf16[512,512]{1,0:T(8,128)(2,1)}, bf16[512,512]{1,0:T(8,128)(2,1)}, ...) | async-done | bytes 1310736 | tf_op jit(solution)/shard_map/psum | solution.py:218
  261.5 2.5 multiply_add_fusion
  (76 shorter events, 22.4 us)
Async XLA Ops:
  7.2 29.9 %all-gather.3.cloned.1.call-start = ((), (), s32[]{:S(2)}) async-start(), calls=%async_computation.5 | async-start | bytes 1802240 | tf_op jit(solution)/shard_map/all_gather | solution.py:18
  11.4 25.6 %copy-start.2 = (f32[2,128,512]{2,1,0:T(8,128)S(1)}, f32[2,128,512]{2,1,0:T(8,128)}, u32[]{:S(2)}) copy-start(f32[2,128,512]{2,1,0:T(8,128)} %param.23) | copy-start | bytes 1572868
  11.5 73.6 %reduce-scatter.4.cloned.1.call-start = ((), (), s32[]{:S(2)}) async-start(), calls=%async_computation.7 | async-start | bytes 2621440 | tf_op jit(solution)/shard_map/reduce_scatter | solution.py:32
  12.6 25.8 %copy-start = (f32[2,512,512]{2,1,0:T(8,128)S(1)}, f32[2,512,512]{2,1,0:T(8,128)}, u32[]{:S(2)}) copy-start(f32[2,512,512]{2,1,0:T(8,128)} %param.22) | copy-start | bytes 6291460
  41.2 0.8 copy-start.3
  55.6 0.7 copy-start.10
  55.6 31.4 %copy-start.12 = (s32[128]{0:T(128)S(1)}, s32[128]{0:T(128)}, u32[]{:S(2)}) copy-start(s32[128]{0:T(128)} %param.21) | copy-start | bytes 1540
  55.6 32.8 %copy-start.11 = (f32[2,512]{1,0:T(2,128)S(1)}, f32[2,512]{1,0:T(2,128)}, u32[]{:S(2)}) copy-start(f32[2,512]{1,0:T(2,128)} %param.27) | copy-start | bytes 12292
  55.6 55.6 %all-gather.5.cloned.1.call-start = ((), (), s32[]{:S(2)}) async-start(), calls=%async_computation.6 | async-start | bytes 1310720 | tf_op jit(solution)/shard_map/all_gather | solution.py:55
  87.0 2.6 copy-start.9
  91.1 9.6 %all-to-all-start = ((f32[4,1,512]{2,1,0:T(1,128)}), f32[4,1,512]{2,1,0:T(1,128)S(1)}, u32[]{:S(2)}, u32[]{:S(2)}) async-start(f32[4,1,512]{2,1,0:T(1,128)} %broadcast_in_dim.10), calls=%async_computation | async-start | bytes 16384 | tf_op jit(solution)/shard_map/all_to_all | solution.py:38
  95.4 79.6 %all-reduce.6.cloned.1.call-start = ((), (), s32[]{:S(2)}) async-start(), calls=%async_computation.8 | async-start | bytes 4194304 | tf_op jit(solution)/shard_map/psum | solution.py:193
  111.2 2.6 copy-start.5
  115.9 8.8 %all-to-all-start.1 = ((f32[4,128,2]{1,2,0:T(2,128)}), f32[4,128,2]{1,2,0:T(2,128)S(1)}, u32[]{:S(2)}, u32[]{:S(2)}) async-start(f32[4,128,2]{1,2,0:T(2,128)} %stack.43), calls=%async_computation.1 | async-start | bytes 8192 | tf_op jit(solution)/shard_map/all_to_all | solution.py:67
  125.3 8.6 %all-to-all-start.2 = ((f32[4,1,1024]{2,1,0:T(1,128)}), f32[4,1,1024]{2,1,0:T(1,128)S(1)}, u32[]{:S(2)}, u32[]{:S(2)}) async-start(f32[4,1,1024]{2,1,0:T(1,128)} %broadcast_in_dim.11), calls=%async_computation.2 | async-start | bytes 32768 | tf_op jit(solution)/shard_map/all_to_all | solution.py:38
  128.6 129.1 %all-reduce.8.cloned.1.call-start = ((), (), s32[]{:S(2)}) async-start(), calls=%async_computation.9 | async-start | bytes 2621440 | tf_op jit(solution)/shard_map/psum | solution.py:218
  133.9 2.6 copy-start.6
  179.6 79.2 %copy-start.4 = (f32[2,128,512]{2,1,0:T(8,128)S(1)}, f32[2,128,512]{2,1,0:T(8,128)}, u32[]{:S(2)}) copy-start(f32[2,128,512]{2,1,0:T(8,128)} %param.26) | copy-start | bytes 1572868
  200.3 11.1 %all-to-all-start.3 = ((f32[4,128,128]{2,1,0:T(8,128)}), f32[4,128,128]{2,1,0:T(8,128)S(1)}, u32[]{:S(2)}, u32[]{:S(2)}) async-start(f32[4,128,128]{2,1,0:T(8,128)} %broadcast_in_dim.12), calls=%async_computation.3 | async-start | bytes 524288 | tf_op jit(solution)/shard_map/all_to_all | solution.py:38
  257.6 2.3 copy-start.7
  257.6 2.3 copy-start.8
  259.9 1.6 copy-start.1
Sparse Core Ops, SparseCore 0:
  11.6 25.4 all-gather.2
  55.7 29.2 reduce-scatter.3
  87.4 23.7 all-gather.4
  115.4 59.5 all-reduce.5
  179.7 77.8 all-reduce.7
